TPU v7x, 512 devices: a whole 4x8x8 slice. The times are simulated.
512 devices in a mesh: node: 8 (over y_hi, core), dp: 64 (over z, y_lo, x).
Axes of the slice: x: 4, y: 8 (y_hi: 4, y_lo: 2; y = y_hi * 2 + y_lo), z: 8, core: 2. Of those that a mesh axis runs over, the one named last changes fastest.
Arguments:
- hidden: bfloat16 [64, 1024, 13824], P('dp', 'node'), may hold values from -6 to 6
- cotangent: bfloat16 [64, 1024, 16], P('dp', 'node'), may hold values from -0.1875 to 0.1875
- momentum: float32 [64, 16, 13824], P('dp', 'node'), may hold values from -6 to 6
- worker_error: float32 [64, 16, 13824], P('dp', 'node'), may hold values from -1.8 to 1.8
- server_error: float32 [16, 13824], P('node', 'dp'), may hold values from -0.3 to 0.3
- master: float32 [16, 13824], P('node'), may hold values from -3 to 3
- second_moment: float32 [16, 13824], P('node'), may hold values from 0.0004 to 0.01
Outputs:
- moment: float32 [64, 16, 13824], P('dp', 'node')
- new_worker_error: float32 [64, 16, 13824], P('dp', 'node')
- new_server_error: float32 [16, 13824], P('node', 'dp')
- weights: bfloat16 [16, 13824], replicated
All inputs are finite; a program needn't handle non-finite values.
Results may differ from a plain program's by a relative error of at most 0.0085.
Values may be sent and summed in bfloat16 or wider, within the bound.
A program may use at most 64 MiB of HBM per device.

v0:
```python
import jax
import jax.numpy as jnp
from jax import lax
from jax.sharding import Mesh
from jax.sharding import PartitionSpec as P

DP = ("dp_0", "dp_1", "dp_2")


beta_one = 0.9
epsilon = 1e-06
learn_rate = 0.5


def cut_along(x, dim, length):
    shape = x.shape
    tiles = x.reshape(*shape[:dim], length, shape[dim] // length, *shape[dim + 1 :])
    return jnp.moveaxis(tiles, dim, 0)


def sent_and_summed(x, axis, dim):
    length = lax.axis_size(axis)
    tiles = lax.all_to_all(cut_along(x, dim, length), axis, 0, 0, tiled=True)
    return jnp.sum(tiles, axis=0)


def laid_out(tiles, dim):
    shape = list(tiles.shape[1:])
    shape[dim] *= tiles.shape[0]
    return jnp.moveaxis(tiles, 0, dim).reshape(shape)


def turned_blocks(tiles, axes, turns):
    inside = tiles.shape[1:]
    result = tiles.reshape(*(lax.axis_size(a) for a in axes), *inside)
    for k in turns:
        result = lax.all_to_all(result, axes[k], k, k, tiled=True)
    return result.reshape(-1, *inside)


def stepwise_exchange(x, axes, turns, split_dim, concat_dim):
    tiles = cut_along(x, split_dim, lax.axis_size(axes))
    return laid_out(turned_blocks(tiles, axes, turns), concat_dim)


def from_everyone(x, axis):
    length = lax.axis_size(axis)
    return lax.all_to_all(jnp.broadcast_to(x[None], (length, *x.shape)), axis, 0, 0, tiled=True)


def gathered_copies(x, axis, dim):
    tiles = from_everyone(x, axis)
    return laid_out(tiles, dim)


def body(hidden, cotangent, momentum, worker_error, server_error, master, second_moment):
    local_acts = hidden[0]
    local_cotan = cotangent[0]
    half_cols = local_acts.shape[1] // 2

    def half_sum(acts_half):
        return sent_and_summed(
            jnp.einsum("tc,tf->cf", local_cotan, acts_half, preferred_element_type=jnp.float32),
            "node",
            0,
        )

    first_half = half_sum(local_acts[:, :half_cols])
    second_half = half_sum(local_acts[:, half_cols:])
    gradient = jnp.concatenate([first_half, second_half], axis=1)
    moment = beta_one * momentum[0] + (1.0 - beta_one) * gradient
    carried = moment + worker_error[0]
    worker_scale = jnp.sqrt(jnp.mean(carried * carried) + epsilon)
    outgoing = (worker_scale * jnp.tanh(carried / worker_scale)).astype(jnp.bfloat16)
    new_worker = carried - outgoing.astype(jnp.float32)
    replicas = lax.axis_size(DP)
    arrived = stepwise_exchange(outgoing[None], DP, (0, 1, 2), 2, 0)
    served = jnp.sum(arrived.astype(jnp.float32), axis=0) / replicas + server_error
    server_scale = jnp.sqrt(jnp.mean(served * served) + epsilon)
    returned = (server_scale * jnp.tanh(served / server_scale)).astype(jnp.bfloat16)
    new_server = served - returned.astype(jnp.float32)
    averaged = gathered_copies(returned, DP, 1)
    update = averaged.astype(jnp.float32) / (jnp.sqrt(second_moment) + 1e-08)
    weight_part = (master - learn_rate * update).astype(jnp.bfloat16)
    weights = gathered_copies(weight_part, "node", 0)
    return (moment[None], new_worker[None], new_server, weights)


def solution(mesh):
    torus = Mesh(
        mesh.devices.reshape(mesh.shape["node"], 8, 2, 4), ("node", "dp_0", "dp_1", "dp_2")
    )
    in_specs = (
        P(DP, "node", None),
        P(DP, "node", None),
        P(DP, "node", None),
        P(DP, "node", None),
        P("node", DP),
        P("node", None),
        P("node", None),
    )
    out_specs = (P(DP, "node", None), P(DP, "node", None), P("node", DP), P())
    return jax.shard_map(body, mesh=torus, in_specs=in_specs, out_specs=out_specs, check_vma=False)
```

profile of v0, /device:TPU:1, one launch (start us, length us, event | category | flops | bytes accessed | tf_op | source)
XLA Modules:
  0.0 121.2 jit_solution(11359461756479638496)
XLA Ops:
  0.7 2.0 %fusion = f32[8,2,6912]{2,0,1:T(8,128)S(1)} fusion(bf16[128,13824]{1,0:T(8,128)(2,1)} %bitcast.29, bf16[8,2,128]{2,1,0:T(2,128)(2,1)} %bitcast.34), kind=kOutput, calls=%fused_computation.1 | convolution fusion | flops 28311552 | bytes 2215936 | tf_op jit(solution)/shard_map/tc,tf->cf/dot_general | solution.py:63
  2.6 1.0 copy.33
  3.6 10.9 %all-to-all-start.1 = ((f32[8,2,6912]{2,1,0:T(2,128)}), f32[8,2,6912]{2,1,0:T(2,128)}, u32[]{:S(2)}, u32[]{:S(2)}) async-start(f32[8,2,6912]{2,1,0:T(2,128)} %copy.33), calls=%async_computation.1 | async-start | bytes 884736 | tf_op jit(solution)/shard_map/all_to_all | solution.py:23
  14.5 0.3 fusion.1
  14.9 1.0 copy.31
  15.9 12.5 %all-to-all-done.1 = f32[8,2,6912]{2,1,0:T(2,128)} async-done(((f32[8,2,6912]{2,1,0:T(2,128)}), f32[8,2,6912]{2,1,0:T(2,128)}, u32[]{:S(2)}, u32[]{:S(2)}) %all-to-all-start.1) | async-done | bytes 442400 | tf_op jit(solution)/shard_map/all_to_all | solution.py:23
  28.3 3.9 %all-to-all-start = ((f32[8,2,6912]{2,1,0:T(2,128)}), f32[8,2,6912]{2,1,0:T(2,128)S(1)}, u32[]{:S(2)}, u32[]{:S(2)}) async-start(f32[8,2,6912]{2,1,0:T(2,128)} %copy.31), calls=%async_computation | async-start | bytes 884736 | tf_op jit(solution)/shard_map/all_to_all | solution.py:23
  32.2 1.1 squeeze.15
  33.4 1.2 reduce_sum.46
  34.5 11.3 %all-to-all-done = f32[8,2,6912]{2,1,0:T(2,128)S(1)} async-done(((f32[8,2,6912]{2,1,0:T(2,128)}), f32[8,2,6912]{2,1,0:T(2,128)S(1)}, u32[]{:S(2)}, u32[]{:S(2)}) %all-to-all-start) | async-done | bytes 442400 | tf_op jit(solution)/shard_map/all_to_all | solution.py:23
  46.0 1.7 %maximum_multiply_fusion.1 = (f32[2,13824]{1,0:T(2,128)S(1)}, f32[]{:T(128)}) fusion(f32[2,6912]{1,0:T(2,128)S(1)} %reduce_sum.46, f32[2,6912]{1,0:T(2,128)S(1)} %reduce_sum.45, f32[1,2,13824]{2,1,0:T(2,128)} %param.10, f32[1,2,13824]{2,1,0:T(2,128)} %param.9), kind=kLoop, calls=%fused_computation.9 | loop fusion | flops 193535 | bytes 442372 | tf_op jit(solution)/shard_map/mul | solution.py:71
  48.3 0.2 mul.97
  48.6 0.8 convert_subtract_fusion
  49.4 0.2 mul.96
  49.8 15.5 %all_to_all.35 = bf16[8,2,4,1,2,216]{5,2,1,4,3,0:T(4,128)(2,1)S(1)} all-to-all(bf16[8,2,4,1,2,216]{5,2,1,4,3,0:T(4,128)(2,1)S(1)} %copy.35), channel_id=1, replica_groups=mesh['node'=8,'dp_0'=8,'dp_1'=2,'dp_2'=4] {'dp_0'}, dimensions={0} | all-to-all | bytes 110592 | tf_op jit(solution)/shard_map/all_to_all | solution.py:37
  65.4 7.8 %all_to_all.36 = bf16[8,2,4,1,2,216]{5,2,0,4,3,1:T(4,128)(2,1)S(1)} all-to-all(bf16[8,2,4,1,2,216]{5,2,0,4,3,1:T(4,128)(2,1)S(1)} %copy.36), channel_id=1, replica_groups=mesh['node'=8,'dp_0'=8,'dp_1'=2,'dp_2'=4] {'dp_1'}, dimensions={1} | all-to-all | bytes 110592 | tf_op jit(solution)/shard_map/all_to_all | solution.py:37
  73.3 8.3 %all_to_all.37 = bf16[8,2,4,1,2,216]{5,1,0,4,3,2:T(2,128)(2,1)S(1)} all-to-all(bf16[8,2,4,1,2,216]{5,1,0,4,3,2:T(2,128)(2,1)S(1)} %copy.37), channel_id=1, replica_groups=mesh['node'=8,'dp_0'=8,'dp_1'=2,'dp_2'=4] {'dp_2'}, dimensions={2} | all-to-all | bytes 110592 | tf_op jit(solution)/shard_map/all_to_all | solution.py:37
  81.6 0.6 multiply_reduce_fusion
  82.9 0.6 convert_subtract_fusion.1
  83.6 13.1 %all_to_all.38 = bf16[64,2,216]{2,1,0:T(2,128)(2,1)S(1)} all-to-all(bf16[64,2,216]{2,1,0:T(2,128)(2,1)S(1)} %broadcast_in_dim.4), channel_id=1, replica_groups=mesh['node'=8,'dp_0'=8,'dp_1'=2,'dp_2'=4] {'dp_0','dp_1','dp_2'}, dimensions={0} | all-to-all | bytes 110592 | tf_op jit(solution)/shard_map/all_to_all | solution.py:48
  97.0 0.2 subtract_convert_fusion
  97.2 0.2 broadcast_in_dim.5
  97.4 22.8 %all_to_all.39 = bf16[8,2,13824]{2,1,0:T(2,128)(2,1)S(1)} all-to-all(bf16[8,2,13824]{2,1,0:T(2,128)(2,1)S(1)} %broadcast_in_dim.5), channel_id=1, replica_groups=mesh['node'=8,'dp_0'=8,'dp_1'=2,'dp_2'=4] {'node'}, dimensions={0} | all-to-all | bytes 884736 | tf_op jit(solution)/shard_map/all_to_all | solution.py:48
  120.3 0.9 reshape.106
  (25 shorter events, 0.8 us)
Async XLA Ops:
  0.6 13.9 %copy-start.5 = (bf16[1,128,16]{1,2,0:T(8,128)(2,1)S(1)}, bf16[1,128,16]{1,2,0:T(8,128)(2,1)}, u32[]{:S(2)}) copy-start(bf16[1,128,16]{1,2,0:T(8,128)(2,1)} %param.8) | copy-start | bytes 12292
  0.6 13.9 %copy-start = (bf16[1,128,13824]{2,1,0:T(8,128)(2,1)S(1)}, bf16[1,128,13824]{2,1,0:T(8,128)(2,1)}, u32[]{:S(2)}) copy-start(bf16[1,128,13824]{2,1,0:T(8,128)(2,1)} %param.7) | copy-start | bytes 10616836
  3.6 24.7 %all-to-all-start.1 = ((f32[8,2,6912]{2,1,0:T(2,128)}), f32[8,2,6912]{2,1,0:T(2,128)}, u32[]{:S(2)}, u32[]{:S(2)}) async-start(f32[8,2,6912]{2,1,0:T(2,128)} %copy.33), calls=%async_computation.1 | async-start | bytes 884736 | tf_op jit(solution)/shard_map/all_to_all | solution.py:23
  14.9 33.7 %copy-start.1 = (f32[1,2,13824]{2,1,0:T(2,128)S(1)}, f32[1,2,13824]{2,1,0:T(2,128)}, u32[]{:S(2)}) copy-start(f32[1,2,13824]{2,1,0:T(2,128)} %param.10) | copy-start | bytes 331780
  14.9 33.7 %copy-start.2 = (f32[1,2,13824]{2,1,0:T(2,128)S(1)}, f32[1,2,13824]{2,1,0:T(2,128)}, u32[]{:S(2)}) copy-start(f32[1,2,13824]{2,1,0:T(2,128)} %param.9) | copy-start | bytes 331780
  14.9 66.8 %copy-start.6 = (f32[2,216]{1,0:T(2,128)S(1)}, f32[2,216]{1,0:T(2,128)}, u32[]{:S(2)}) copy-start(f32[2,216]{1,0:T(2,128)} %param.11) | copy-start | bytes 5188
  14.9 82.1 %copy-start.3 = (f32[2,13824]{1,0:T(2,128)S(1)}, f32[2,13824]{1,0:T(2,128)}, u32[]{:S(2)}) copy-start(f32[2,13824]{1,0:T(2,128)} %param.12) | copy-start | bytes 331780
  14.9 82.1 %copy-start.4 = (f32[2,13824]{1,0:T(2,128)S(1)}, f32[2,13824]{1,0:T(2,128)}, u32[]{:S(2)}) copy-start(f32[2,13824]{1,0:T(2,128)} %param.13) | copy-start | bytes 331780
  28.3 17.4 %all-to-all-start = ((f32[8,2,6912]{2,1,0:T(2,128)}), f32[8,2,6912]{2,1,0:T(2,128)S(1)}, u32[]{:S(2)}, u32[]{:S(2)}) async-start(f32[8,2,6912]{2,1,0:T(2,128)} %copy.31), calls=%async_computation | async-start | bytes 884736 | tf_op jit(solution)/shard_map/all_to_all | solution.py:23
where the time goes:
time: 122 us; the launch traced here: 121 us
  blocking collectives  67.6 us (55%)
  waiting for transfers between devices  23.7 us (19%)
  starting transfers between devices  14.8 us (12%)
  other arithmetic  5.44 us (4%)
  local copies, waits for them, and re-layouts  5.16 us (4%)
  matrix products  2.33 us (2%)
  between operations  2.2 us (2%)
    all_to_all x2, blocking collectives, from_everyone(): lax.all_to_all(jnp.broadcast_to(x[None], (length, *x.shape)), axis, 0, 0,...  36 us
    all_to_all x3, blocking collectives, turned_blocks(): result = lax.all_to_all(result, axes[k], k, k, tiled=True)  31.6 us
    all_to_all x2, waiting for transfers between devices, sent_and_summed(): tiles = lax.all_to_all(cut_along(x, dim, length), axis, 0, 0, tiled=True)  23.7 us
    all_to_all x2, starting transfers between devices, sent_and_summed(): tiles = lax.all_to_all(cut_along(x, dim, length), axis, 0, 0, tiled=True)  14.8 us
  transfers between devices with their start and end apart: 2, of which 2 were waited for; matrix products, arithmetic and copies ran while one was open for 3% of the time, Pallas kernels for 0%

commit v1 on v0

v1 whole, which is shorter than its diff:
```python
import functools

import jax
import jax.numpy as jnp
from jax import lax
from jax.experimental import pallas as pl
from jax.experimental.pallas import tpu as pltpu
from jax.sharding import PartitionSpec as P

MESH = pl.DeviceIdType.MESH
F32 = jnp.float32
BF16 = jnp.bfloat16

FF = 13824
LANES = 128
GROUPS = FF // LANES
DENSE = 2 * GROUPS
PADDED = 224
SERVERS = 64
PIECE = FF // SERVERS
QUARTER = GROUPS // 4
BETA = 0.9
EPSILON = 1e-6
RATE = 0.5


def far_first(j, half):
    odd = lax.rem(j, 2)
    return half + (1 - odd) * (j // 2) - odd * ((j + 1) // 2)


def device(x, y, z, c):
    return ((y // 2) * 2 + c, z * 8 + lax.rem(y, 2) * 4 + x)


def kernel(
    hid, cot, mom, werr, serr, mast, second,
    moment_out, werr_out, serr_out, weights_out,
    hid_v, part, core_in, y_out, y_in, mom_v, werr_v, mast_v, second_v, serr_v,
    sent_v, pieces, arrived, wpiece, gathered, wall, spread,
    load_sem, store_sem, core_send, core_recv, y_send, y_recv, ready,
    b_send, b_recv, c_send, c_recv, x_send, x_recv, s_send, s_recv,
):
    node = lax.axis_index("node")
    dp = lax.axis_index("dp")
    c = lax.rem(node, 2)
    yh = node // 2
    z = dp // 8
    yl = lax.rem(dp // 4, 2)
    x = lax.rem(dp, 4)
    y = yh * 2 + yl
    sibling = (node + 1 - 2 * c, dp)

    loads = [
        pltpu.make_async_copy(
            hid.at[:, pl.ds(j * QUARTER * LANES, QUARTER * LANES)],
            hid_v.at[:, pl.ds(j * QUARTER * LANES, QUARTER * LANES)],
            load_sem.at[j],
        )
        for j in range(4)
    ]
    states = [
        pltpu.make_async_copy(mom.reshape(DENSE, LANES), mom_v.at[pl.ds(0, DENSE)], load_sem.at[4]),
        pltpu.make_async_copy(werr.reshape(DENSE, LANES), werr_v.at[pl.ds(0, DENSE)], load_sem.at[5]),
        pltpu.make_async_copy(mast, mast_v.at[pl.ds(0, GROUPS)], load_sem.at[6]),
        pltpu.make_async_copy(second, second_v.at[pl.ds(0, GROUPS)], load_sem.at[7]),
    ]
    for load in loads:
        load.start()

    barrier = pltpu.get_barrier_semaphore()

    def greet(who):
        pl.semaphore_signal(barrier, 1, device_id=who, device_id_type=MESH)

    @pl.loop(0, 7)
    def _(j):
        greet(device(x, y, lax.rem(z + far_first(j, 4), 8), c))
        greet(device(x, lax.rem(y + far_first(j, 4), 8), z, c))

    @pl.loop(1, 4)
    def _(j):
        other = lax.rem(x + j, 4)
        greet(device(other, y, z, c))
        greet(device(other, yh * 2 + 1 - yl, z, c))

    greet(sibling)

    for state in states:
        state.start()

    tail = jnp.zeros((PADDED - DENSE, LANES), F32)
    for a in range(2):
        for b in range(4):
            part[a, b, pl.ds(DENSE, PADDED - DENSE), :] = tail
    mom_v[pl.ds(DENSE, PADDED - DENSE), :] = tail
    werr_v[pl.ds(DENSE, PADDED - DENSE), :] = tail
    mast_v[pl.ds(GROUPS, 4)] = jnp.zeros((4, 2, LANES), F32)
    second_v[pl.ds(GROUPS, 4)] = jnp.zeros((4, 2, LANES), F32)
    serr_v[...] = jnp.zeros((4, LANES), F32)
    serr_v[pl.ds(0, 2), :] = serr[:, pl.ds(0, LANES)]
    serr_v[pl.ds(2, 2), pl.ds(0, PIECE - LANES)] = serr[:, pl.ds(LANES, PIECE - LANES)]

    cot_value = cot[...]
    for j in range(4):
        loads[j].wait()
        sums = jnp.dot(
            cot_value,
            hid_v[:, pl.ds(j * QUARTER * LANES, QUARTER * LANES)],
            preferred_element_type=F32,
        )
        for g in range(QUARTER):
            row = 2 * (j * QUARTER + g)
            for n in range(8):
                part[n % 2, n // 2, pl.ds(row, 2), :] = sums[
                    2 * n : 2 * n + 2, g * LANES : (g + 1) * LANES
                ]

    pl.semaphore_wait(barrier, 21)

    def to_core(d):
        return pltpu.make_async_remote_copy(
            part.at[1 - c, lax.rem(yh + d, 4)], core_in.at[d], core_send.at[d], core_recv.at[d],
            device_id=sibling, device_id_type=MESH,
        )

    def to_node(d):
        return pltpu.make_async_remote_copy(
            y_out.at[d - 1], y_in.at[d - 1], y_send.at[d - 1], y_recv.at[d - 1],
            device_id=(lax.rem(yh + d, 4) * 2 + c, dp), device_id_type=MESH,
        )

    for d in (2, 1, 3, 0):
        to_core(d).start()

    @pl.loop(0, 7)
    def _(j):
        pl.semaphore_signal(
            ready, 1, device_id=device(x, y, lax.rem(z + far_first(j, 4), 8), c), device_id_type=MESH
        )

    for d in (2, 1, 3):
        to_core(d).wait_recv()
        y_out[d - 1] = (part[c, lax.rem(yh + d, 4)] + core_in[d]).astype(BF16)
        to_node(d).start()
    to_core(0).wait_recv()
    gradient = part[c, yh] + core_in[0]
    states[0].wait()
    states[1].wait()
    for d in (1, 3, 2):
        to_node(d).wait_recv()
        gradient = gradient + y_in[d - 1].astype(F32)

    moment = BETA * mom_v[...] + (1.0 - BETA) * gradient
    carried = moment + werr_v[...]
    mom_v[...] = moment
    square = jnp.sum(carried * carried, axis=(0, 1), keepdims=True)
    scale = jnp.sqrt(square / (2 * FF) + EPSILON)
    sent = (scale * jnp.tanh(carried / scale)).astype(BF16).astype(F32)
    sent_v[...] = sent
    werr_v[...] = carried - sent

    lane = lax.broadcasted_iota(jnp.int32, (8, LANES), 1)
    for p in range(SERVERS):
        group, shift = divmod(PIECE * p, LANES)
        rows = sent_v[pl.ds(2 * group, 8), :]
        if shift:
            first = pltpu.roll(rows, LANES - shift, 1)
            rows = jnp.where(lane < LANES - shift, first, pltpu.roll(first, 6, 0))
        pieces[p] = rows[0:4]

    pl.semaphore_wait(ready, 7)

    def to_server(k):
        jz, jx, jy = k // 8, lax.rem(k, 8) // 2, lax.rem(k, 2)
        tz = lax.rem(z + far_first(jz, 4), 8)
        tx = lax.rem(x + far_first(jx, 2), 4)
        ty = lax.rem(yl + 1 - jy, 2)
        target = tz * 8 + ty * 4 + tx
        return pltpu.make_async_remote_copy(
            pieces.at[target], arrived.at[dp], b_send, b_recv, device_id=(node, target), device_id_type=MESH
        )

    @pl.loop(0, SERVERS - 1)
    def _(k):
        to_server(k).start()

    arrived[dp] = pieces[dp]
    moment_store = pltpu.make_async_copy(mom_v.at[pl.ds(0, DENSE)], moment_out.reshape(DENSE, LANES), store_sem.at[0])
    werr_store = pltpu.make_async_copy(werr_v.at[pl.ds(0, DENSE)], werr_out.reshape(DENSE, LANES), store_sem.at[1])
    moment_store.start()
    werr_store.start()

    states[2].wait()
    states[3].wait()
    column = dp * PIECE
    group, shift = column // LANES, lax.rem(column, LANES)

    def own_piece(ref):
        rows = jnp.concatenate([ref[group + j] for j in range(4)], axis=0)
        first = pltpu.roll(rows, lax.rem(LANES - shift, LANES), 1)
        return jnp.where(lane < LANES - shift, first, pltpu.roll(first, 6, 0))[0:4]

    row4 = lax.broadcasted_iota(jnp.int32, (4, LANES), 0)
    lane4 = lax.broadcasted_iota(jnp.int32, (4, LANES), 1)
    valid = (row4 < 2) | (lane4 < PIECE - LANES)
    own_master = own_piece(mast_v)
    divisor = jnp.sqrt(jnp.where(valid, own_piece(second_v), 1.0)) + 1e-8

    everyone = SERVERS - 1
    pltpu.make_async_copy(pieces.at[pl.ds(0, everyone)], arrived.at[pl.ds(0, everyone)], b_recv).wait()
    served = jnp.sum(arrived[...], axis=0) / SERVERS + serr_v[...]
    served = jnp.where(valid, served, 0.0)
    square = jnp.sum(served * served, axis=(0, 1), keepdims=True)
    scale = jnp.sqrt(square / (2 * PIECE) + EPSILON)
    returned = (scale * jnp.tanh(served / scale)).astype(BF16).astype(F32)
    updated = own_master - RATE * (returned / divisor)
    updated = jnp.concatenate([updated[0:1], updated[2:3], updated[1:2], updated[3:4]], axis=0)
    wpiece[...] = updated.astype(BF16).astype(F32)

    slot = (z * 2 + yl) * 4 + yh

    def to_plane(k):
        tz = lax.rem(z + far_first(k // 8, 4), 8)
        ty = lax.rem(y + far_first(lax.rem(k, 8), 4), 8)
        return pltpu.make_async_remote_copy(
            wpiece, gathered.at[slot], c_send, c_recv, device_id=device(x, ty, tz, c), device_id_type=MESH
        )

    @pl.loop(0, SERVERS - 1)
    def _(k):
        to_plane(k).start()

    gathered[slot] = wpiece[...]
    residual = served - returned
    serr_out[:, pl.ds(0, LANES)] = residual[0:2]
    serr_out[:, pl.ds(LANES, PIECE - LANES)] = residual[2:4, 0 : PIECE - LANES]

    pltpu.make_async_copy(pieces.at[pl.ds(0, everyone)], gathered.at[pl.ds(0, everyone)], c_recv).wait()
    wall[c, x] = gathered[...].reshape(4 * SERVERS, LANES).astype(BF16)

    def to_x(d):
        return pltpu.make_async_remote_copy(
            wall.at[c, x], wall.at[c, x], x_send.at[d - 1], x_recv.at[d - 1],
            device_id=(node, dp - x + lax.rem(x + d, 4)), device_id_type=MESH,
        )

    def from_x(d):
        block = wall.at[c, lax.rem(x + 4 - d, 4)]
        return pltpu.make_async_remote_copy(
            block, block, x_send.at[d - 1], x_recv.at[d - 1],
            device_id=(node, dp - x + lax.rem(x + d, 4)), device_id_type=MESH,
        )

    def to_sibling(d):
        block = wall.at[c, lax.rem(x + 4 - d, 4)]
        return pltpu.make_async_remote_copy(
            block, block, s_send.at[d], s_recv.at[d], device_id=sibling, device_id_type=MESH
        )

    def from_sibling(d):
        block = wall.at[1 - c, lax.rem(x + 4 - d, 4)]
        return pltpu.make_async_remote_copy(
            block, block, s_send.at[d], s_recv.at[d], device_id=sibling, device_id_type=MESH
        )

    for d in (2, 1, 3):
        to_x(d).start()
    to_sibling(0).start()
    for d in (1, 3, 2):
        from_x(d).wait_recv()
        to_sibling(d).start()
    for d in (0, 1, 3, 2):
        from_sibling(d).wait_recv()

    @pl.loop(0, 4)
    def _(q):
        parts = [[] for _ in range(QUARTER)]
        for pp in range(16):
            for core in range(2):
                block = wall[core, pp % 4, pl.ds(pl.multiple_of(q * 64 + 16 * (pp // 4), 16), 16), :].astype(F32)
                for h in range(4):
                    spread[pp, pl.ds(8 * h + 4 * core, 4), :] = block[4 * h : 4 * h + 4]
            for half in range(2):
                rows = [spread[pp, pl.ds(16 * h + half, 8, stride=2), :] for h in range(2)]
                begin = PIECE * pp + LANES * half
                end = min(begin + LANES, PIECE * (pp + 1))
                group, shift = divmod(begin, LANES)
                if shift:
                    rows = [pltpu.roll(r, shift, 1) for r in rows]
                for g in (group, group + 1):
                    if max(begin, g * LANES) < min(end, (g + 1) * LANES):
                        parts[g].append((max(begin, g * LANES) - g * LANES, rows))
        for g in range(QUARTER):
            total = parts[g][0][1]
            for low, rows in parts[g][1:]:
                total = [jnp.where(lane < low, t, r) for t, r in zip(total, rows)]
            weights_out[:, pl.ds(pl.multiple_of(q * QUARTER * LANES + g * LANES, LANES), LANES)] = (
                jnp.concatenate(total, axis=0).astype(BF16)
            )

    moment_store.wait()
    werr_store.wait()
    for d in range(4):
        to_core(d).wait_send()
        to_sibling(d).wait_send()
    for d in range(1, 4):
        to_node(d).wait_send()
        to_x(d).wait_send()
    pltpu.make_async_copy(pieces.at[pl.ds(0, everyone)], arrived.at[pl.ds(0, everyone)], b_send).wait()
    pltpu.make_async_copy(pieces.at[pl.ds(0, everyone)], gathered.at[pl.ds(0, everyone)], c_send).wait()


def grouped(a):
    return a.reshape(2, GROUPS, LANES).transpose(1, 0, 2)


def body(hidden, cotangent, momentum, worker_error, server_error, master, second_moment):
    anywhere = pl.BlockSpec(memory_space=pl.ANY)
    vmem = pl.BlockSpec(memory_space=pltpu.VMEM)
    dma = pltpu.SemaphoreType.DMA
    moment, werr, serr, weights = pl.pallas_call(
        kernel,
        out_shape=[
            jax.ShapeDtypeStruct((GROUPS, 2, LANES), F32),
            jax.ShapeDtypeStruct((GROUPS, 2, LANES), F32),
            jax.ShapeDtypeStruct((2, PIECE), F32),
            jax.ShapeDtypeStruct((16, FF), BF16),
        ],
        in_specs=[anywhere, vmem, anywhere, anywhere, vmem, anywhere, anywhere],
        out_specs=[anywhere, anywhere, vmem, vmem],
        scratch_shapes=[
            pltpu.VMEM((128, FF), BF16),
            pltpu.VMEM((2, 4, PADDED, LANES), F32),
            pltpu.VMEM((4, PADDED, LANES), F32),
            pltpu.VMEM((3, PADDED, LANES), BF16),
            pltpu.VMEM((3, PADDED, LANES), BF16),
            pltpu.VMEM((PADDED, LANES), F32),
            pltpu.VMEM((PADDED, LANES), F32),
            pltpu.VMEM((GROUPS + 4, 2, LANES), F32),
            pltpu.VMEM((GROUPS + 4, 2, LANES), F32),
            pltpu.VMEM((4, LANES), F32),
            pltpu.VMEM((PADDED, LANES), F32),
            pltpu.VMEM((SERVERS, 4, LANES), F32),
            pltpu.VMEM((SERVERS, 4, LANES), F32),
            pltpu.VMEM((4, LANES), F32),
            pltpu.VMEM((SERVERS, 4, LANES), F32),
            pltpu.VMEM((2, 4, 4 * SERVERS, LANES), BF16),
            pltpu.VMEM((16, 32, LANES), F32),
            dma((8,)), dma((2,)), dma((4,)), dma((4,)), dma((3,)), dma((3,)),
            pltpu.SemaphoreType.REGULAR,
            dma, dma, dma, dma, dma((3,)), dma((3,)), dma((4,)), dma((4,)),
        ],
        compiler_params=pltpu.CompilerParams(
            collective_id=0, has_side_effects=True, vmem_limit_bytes=60 * 1024 * 1024
        ),
        cost_estimate=pl.CostEstimate(flops=2 * 128 * 16 * FF, bytes_accessed=5_000_000, transcendentals=2 * FF),
        name="compressed_step",
    )(
        hidden[0],
        cotangent[0].T,
        grouped(momentum),
        grouped(worker_error),
        server_error,
        grouped(master),
        grouped(second_moment),
    )

    def rows_of(a):
        return a.transpose(1, 0, 2).reshape(1, 2, FF)

    return rows_of(moment), rows_of(werr), serr, weights


def solution(mesh):
    in_specs = (
        P("dp", "node", None),
        P("dp", "node", None),
        P("dp", "node", None),
        P("dp", "node", None),
        P("node", "dp"),
        P("node", None),
        P("node", None),
    )
    out_specs = (P("dp", "node", None), P("dp", "node", None), P("node", "dp"), P())
    return jax.shard_map(body, mesh=mesh, in_specs=in_specs, out_specs=out_specs, check_vma=False)
```

time: 122 us -> 53.7 us (0.44)
  blocking collectives: 67.6 us -> 0 us
  Pallas kernels: 0 us -> 46.6 us
  waiting for transfers between devices: 23.7 us -> 0 us
  starting transfers between devices: 14.8 us -> 0 us
  other arithmetic: 5.44 us -> 0 us
  matrix products: 2.33 us -> 0 us
  between operations: 2.2 us -> 0.64 us
    all_to_all x5 -> x0, blocking collectives: 67.6 us -> none  [the longest x2 36 us: from_everyone(): lax.all_to_all(jnp.broadcast_to(x[None], (length, *x.shape)), axis, 0, 0,...]
    pallas_call x0 -> x1, Pallas kernels: none -> 46.6 us  [body(): pl.pallas_call(kernel, out_shape=[jax.ShapeDtypeStruct((GROUPS, 2, LANES)...]
    all_to_all x2 -> x0, waiting for transfers between devices: 23.7 us -> none  [sent_and_summed(): tiles = lax.all_to_all(cut_along(x, dim, length), axis, 0, 0, tiled=True)]
    all_to_all x2 -> x0, starting transfers between devices: 14.8 us -> none  [sent_and_summed(): tiles = lax.all_to_all(cut_along(x, dim, length), axis, 0, 0, tiled=True)]
    unnamed x14 -> x4, local copies, waits for them, and re-layouts: 0.03 us -> 6.14 us
    dot_general x2 -> x0, matrix products: 2.33 us -> none  [half_sum(): jnp.einsum('tc,tf->cf', local_cotan, acts_half, preferred_element_type=jn...]
    reduce_sum x4 -> x0, other arithmetic: 2.02 us -> none  [the longest x2 1.33 us: sent_and_summed(): return jnp.sum(tiles, axis=0)]
    dot_general x2 -> x0, local copies, waits for them, and re-layouts: 2 us -> none  [half_sum(): jnp.einsum('tc,tf->cf', local_cotan, acts_half, preferred_element_type=jn...]
  transfers between devices with their start and end apart: 2 -> 0, of which waited for: 2 -> 0; matrix products, arithmetic and copies ran while one was open for 3% -> 0% of each run, Pallas kernels for 0% -> 0%
where the time goes in v1:
time: 53.7 us; the launch traced here: 53.4 us
  Pallas kernels  46.6 us (87%)
  local copies, waits for them, and re-layouts  6.14 us (11%)
  between operations  0.64 us (1%)
    pallas_call x1, Pallas kernels, body(): pl.pallas_call(kernel, out_shape=[jax.ShapeDtypeStruct((GROUPS, 2, LANES)...  46.6 us
    unnamed x4, local copies, waits for them, and re-layouts  6.14 us

profile of v1, /device:TPU:1, one launch (start us, length us, event | category | flops | bytes accessed | tf_op | source)
XLA Modules:
  0.0 53.4 jit_solution(12887756433697897352)
XLA Ops:
  0.6 46.6 %compressed_step.1 = (f32[108,2,128]{2,1,0:T(2,128)}, f32[108,2,128]{2,1,0:T(2,128)}, f32[2,216]{1,0:T(2,128)}, bf16[16,13824]{1,0:T(8,128)(2,1)}) custom-call(bf16[128,13824]{1,0:T(8,128)(2,1)} %bitcast.22, bf16[16,128]{1,0:T(8,128)(2,1)} %bitcast.29, f32[108,2,128]{2,1,0:T(2,128)} %bitcast.25, f32[108,2,128]{2,1,0:T(2,128)} %bitcast.26, f32[2,216]{1,0:T(2,128)} %serr.1, ...), custom_call_target="tpu_custom_call" | custom-call | flops 56623104 | bytes 5000000 | tf_op jit(solution)/shard_map/compressed_step/pallas_call | solution.py:322
  47.3 1.5 %copy.15 = f32[1,2,13824]{2,1,0:T(2,128)} copy(f32[1,2,13824]{2,1,0:T(2,128)} %bitcast.24) | data formatting | bytes 221184
  48.8 1.5 %copy.16 = f32[1,2,13824]{2,1,0:T(2,128)} copy(f32[1,2,13824]{2,1,0:T(2,128)} %bitcast.23) | data formatting | bytes 221184
  50.4 1.2 %copy.17 = f32[2,216]{1,0:T(2,128)} copy(f32[2,216]{1,0:T(2,128)} %get-tuple-element.18) | data formatting | bytes 3456
  51.6 1.8 %copy.18 = bf16[16,13824]{1,0:T(8,128)(2,1)} copy(bf16[16,13824]{1,0:T(8,128)(2,1)} %get-tuple-element.19) | data formatting | bytes 884736

commit v2 on v1

--- a/solution.py
+++ b/solution.py
@@ -311,6 +311,15 @@
     pltpu.make_async_copy(pieces.at[pl.ds(0, everyone)], gathered.at[pl.ds(0, everyone)], c_send).wait()
 
 
+def finish(*refs):
+    sems = refs[8]
+    copies = [pltpu.make_async_copy(refs[i], refs[4 + i], sems.at[i]) for i in (3, 0, 1, 2)]
+    for copy in copies:
+        copy.start()
+    for copy in copies:
+        copy.wait()
+
+
 def grouped(a):
     return a.reshape(2, GROUPS, LANES).transpose(1, 0, 2)
 
@@ -322,10 +331,10 @@
     moment, werr, serr, weights = pl.pallas_call(
         kernel,
         out_shape=[
-            jax.ShapeDtypeStruct((GROUPS, 2, LANES), F32),
-            jax.ShapeDtypeStruct((GROUPS, 2, LANES), F32),
-            jax.ShapeDtypeStruct((2, PIECE), F32),
-            jax.ShapeDtypeStruct((16, FF), BF16),
+            pltpu.VMEM((GROUPS, 2, LANES), F32),
+            pltpu.VMEM((GROUPS, 2, LANES), F32),
+            pltpu.VMEM((2, PIECE), F32),
+            pltpu.VMEM((16, FF), BF16),
         ],
         in_specs=[anywhere, vmem, anywhere, anywhere, vmem, anywhere, anywhere],
         out_specs=[anywhere, anywhere, vmem, vmem],
@@ -366,6 +375,16 @@
         grouped(second_moment),
     )
 
+    moment, werr, serr, weights = pl.pallas_call(
+        finish,
+        out_shape=[jax.ShapeDtypeStruct(a.shape, a.dtype) for a in (moment, werr, serr, weights)],
+        in_specs=[anywhere] * 4,
+        out_specs=[anywhere] * 4,
+        scratch_shapes=[dma((4,))],
+        compiler_params=pltpu.CompilerParams(vmem_limit_bytes=1024 * 1024),
+        name="finish",
+    )(moment, werr, serr, weights)
+
     def rows_of(a):
         return a.transpose(1, 0, 2).reshape(1, 2, FF)
 

time: 53.7 us -> 47.5 us (0.88)
  local copies, waits for them, and re-layouts: 6.14 us -> 0 us
    unnamed x4 -> x0, local copies, waits for them, and re-layouts: 6.14 us -> none
    pallas_call x1 -> x2, Pallas kernels: 46.6 us -> 46.7 us  [the longest x1 45.8 us: body(): pl.pallas_call(kernel, out_shape=[pltpu.VMEM((GROUPS, 2, LANES), F32), pl...]
where the time goes in v2:
time: 47.5 us; the launch traced here: 47.4 us
  Pallas kernels  46.7 us (98%)
  between operations  0.64 us (1%)
    pallas_call x1, Pallas kernels, body(): pl.pallas_call(kernel, out_shape=[pltpu.VMEM((GROUPS, 2, LANES), F32), pl...  45.8 us

profile of v2, /device:TPU:1, one launch (start us, length us, event | category | flops | bytes accessed | tf_op | source)
XLA Modules:
  0.0 47.4 jit_solution(5646817692510367953)
XLA Ops:
  0.6 45.8 %compressed_step.1 = (f32[108,2,128]{2,1,0:T(2,128)S(1)}, f32[108,2,128]{2,1,0:T(2,128)S(1)}, f32[2,216]{1,0:T(2,128)S(1)}, bf16[16,13824]{1,0:T(8,128)(2,1)S(1)}) custom-call(bf16[128,13824]{1,0:T(8,128)(2,1)} %bitcast.22, bf16[16,128]{1,0:T(8,128)(2,1)} %bitcast.27, f32[108,2,128]{2,1,0:T(2,128)} %bitcast.23, f32[108,2,128]{2,1,0:T(2,128)} %bitcast.24, ...), custom_call_target="tpu_custom_call" | custom-call | flops 56623104 | bytes 5000000 | tf_op jit(solution)/shard_map/compressed_step/pallas_call | solution.py:331
  46.5 0.9 %finish.1 = (f32[108,2,128]{2,1,0:T(2,128)}, f32[108,2,128]{2,1,0:T(2,128)}, f32[2,216]{1,0:T(2,128)}, bf16[16,13824]{1,0:T(8,128)(2,1)}) custom-call(f32[108,2,128]{2,1,0:T(2,128)S(1)} %get-tuple-element.12.refs_0_, f32[108,2,128]{2,1,0:T(2,128)S(1)} %get-tuple-element.13.refs_1_, f32[2,216]{1,0:T(2,128)S(1)} %get-tuple-element.14.refs_2_, ...), custom_call_target="tpu_custom_call" | custom-call | tf_op jit(solution)/shard_map/finish/pallas_call | solution.py:378

commit v3 on v2

--- a/solution.py
+++ b/solution.py
@@ -37,7 +37,7 @@
     hid, cot, mom, werr, serr, mast, second,
     moment_out, werr_out, serr_out, weights_out,
     hid_v, part, core_in, y_out, y_in, mom_v, werr_v, mast_v, second_v, serr_v,
-    sent_v, pieces, arrived, wpiece, gathered, wall, spread,
+    sent_v, pieces, arrived, wpiece, wall, spread,
     load_sem, store_sem, core_send, core_recv, y_send, y_recv, ready,
     b_send, b_recv, c_send, c_recv, x_send, x_recv, s_send, s_recv,
 ):
@@ -156,7 +156,7 @@
     mom_v[...] = moment
     square = jnp.sum(carried * carried, axis=(0, 1), keepdims=True)
     scale = jnp.sqrt(square / (2 * FF) + EPSILON)
-    sent = (scale * jnp.tanh(carried / scale)).astype(BF16).astype(F32)
+    sent = (scale * jnp.tanh(carried * (1.0 / scale))).astype(BF16).astype(F32)
     sent_v[...] = sent
     werr_v[...] = carried - sent
 
@@ -167,7 +167,7 @@
         if shift:
             first = pltpu.roll(rows, LANES - shift, 1)
             rows = jnp.where(lane < LANES - shift, first, pltpu.roll(first, 6, 0))
-        pieces[p] = rows[0:4]
+        pieces[p] = rows[0:4].astype(BF16)
 
     pl.semaphore_wait(ready, 7)
 
@@ -181,7 +181,7 @@
             pieces.at[target], arrived.at[dp], b_send, b_recv, device_id=(node, target), device_id_type=MESH
         )
 
-    @pl.loop(0, SERVERS - 1)
+    @pl.loop(0, SERVERS - 1, unroll=7)
     def _(k):
         to_server(k).start()
 
@@ -205,82 +205,72 @@
     lane4 = lax.broadcasted_iota(jnp.int32, (4, LANES), 1)
     valid = (row4 < 2) | (lane4 < PIECE - LANES)
     own_master = own_piece(mast_v)
-    divisor = jnp.sqrt(jnp.where(valid, own_piece(second_v), 1.0)) + 1e-8
-
-    everyone = SERVERS - 1
-    pltpu.make_async_copy(pieces.at[pl.ds(0, everyone)], arrived.at[pl.ds(0, everyone)], b_recv).wait()
-    served = jnp.sum(arrived[...], axis=0) / SERVERS + serr_v[...]
+    step = RATE / (jnp.sqrt(jnp.where(valid, own_piece(second_v), 1.0)) + 1e-8)
+
+    others = pl.ds(0, SERVERS - 1)
+    pltpu.make_async_copy(arrived.at[others], arrived.at[others], b_recv).wait()
+    served = jnp.sum(arrived[...].astype(F32), axis=0) / SERVERS + serr_v[...]
     served = jnp.where(valid, served, 0.0)
     square = jnp.sum(served * served, axis=(0, 1), keepdims=True)
     scale = jnp.sqrt(square / (2 * PIECE) + EPSILON)
     returned = (scale * jnp.tanh(served / scale)).astype(BF16).astype(F32)
-    updated = own_master - RATE * (returned / divisor)
+    updated = own_master - step * returned
     updated = jnp.concatenate([updated[0:1], updated[2:3], updated[1:2], updated[3:4]], axis=0)
-    wpiece[...] = updated.astype(BF16).astype(F32)
-
-    slot = (z * 2 + yl) * 4 + yh
+    wpiece[...] = updated.astype(BF16)
+
+    slot = yl * 4 + yh
 
     def to_plane(k):
-        tz = lax.rem(z + far_first(k // 8, 4), 8)
+        dz = far_first(k // 8, 4)
         ty = lax.rem(y + far_first(lax.rem(k, 8), 4), 8)
         return pltpu.make_async_remote_copy(
-            wpiece, gathered.at[slot], c_send, c_recv, device_id=device(x, ty, tz, c), device_id_type=MESH
-        )
-
-    @pl.loop(0, SERVERS - 1)
+            wpiece, wall.at[c, x, z, slot], c_send, c_recv.at[dz],
+            device_id=device(x, ty, lax.rem(z + dz, 8), c), device_id_type=MESH,
+        )
+
+    @pl.loop(0, SERVERS - 1, unroll=7)
     def _(k):
         to_plane(k).start()
 
-    gathered[slot] = wpiece[...]
+    wall[c, x, z, slot] = wpiece[...]
     residual = served - returned
     serr_out[:, pl.ds(0, LANES)] = residual[0:2]
     serr_out[:, pl.ds(LANES, PIECE - LANES)] = residual[2:4, 0 : PIECE - LANES]
 
-    pltpu.make_async_copy(pieces.at[pl.ds(0, everyone)], gathered.at[pl.ds(0, everyone)], c_recv).wait()
-    wall[c, x] = gathered[...].reshape(4 * SERVERS, LANES).astype(BF16)
-
-    def to_x(d):
-        return pltpu.make_async_remote_copy(
-            wall.at[c, x], wall.at[c, x], x_send.at[d - 1], x_recv.at[d - 1],
+    def to_x(d, source):
+        block = wall.at[c, x, source]
+        return pltpu.make_async_remote_copy(
+            block, block, x_send, x_recv.at[d - 1],
             device_id=(node, dp - x + lax.rem(x + d, 4)), device_id_type=MESH,
         )
 
-    def from_x(d):
+    def to_sibling(block):
+        return pltpu.make_async_remote_copy(
+            block, block, s_send, s_recv, device_id=sibling, device_id_type=MESH
+        )
+
+    for dz in (0, 1, 7, 2, 6, 3, 5, 4):
+        source = lax.rem(z + 8 - dz, 8)
+        landed = wall.at[c, x, source, pl.ds(0, 8 if dz else 7)]
+        pltpu.make_async_copy(landed, landed, c_recv.at[dz]).wait()
+        for d in (2, 1, 3):
+            to_x(d, source).start()
+        to_sibling(wall.at[c, x, source]).start()
+    for d in (1, 3, 2):
         block = wall.at[c, lax.rem(x + 4 - d, 4)]
-        return pltpu.make_async_remote_copy(
-            block, block, x_send.at[d - 1], x_recv.at[d - 1],
-            device_id=(node, dp - x + lax.rem(x + d, 4)), device_id_type=MESH,
-        )
-
-    def to_sibling(d):
-        block = wall.at[c, lax.rem(x + 4 - d, 4)]
-        return pltpu.make_async_remote_copy(
-            block, block, s_send.at[d], s_recv.at[d], device_id=sibling, device_id_type=MESH
-        )
-
-    def from_sibling(d):
-        block = wall.at[1 - c, lax.rem(x + 4 - d, 4)]
-        return pltpu.make_async_remote_copy(
-            block, block, s_send.at[d], s_recv.at[d], device_id=sibling, device_id_type=MESH
-        )
-
-    for d in (2, 1, 3):
-        to_x(d).start()
-    to_sibling(0).start()
-    for d in (1, 3, 2):
-        from_x(d).wait_recv()
-        to_sibling(d).start()
-    for d in (0, 1, 3, 2):
-        from_sibling(d).wait_recv()
+        pltpu.make_async_copy(block, block, x_recv.at[d - 1]).wait()
+        to_sibling(block).start()
+    pltpu.make_async_copy(wall.at[1 - c], wall.at[1 - c], s_recv).wait()
 
     @pl.loop(0, 4)
     def _(q):
         parts = [[] for _ in range(QUARTER)]
         for pp in range(16):
             for core in range(2):
-                block = wall[core, pp % 4, pl.ds(pl.multiple_of(q * 64 + 16 * (pp // 4), 16), 16), :].astype(F32)
                 for h in range(4):
-                    spread[pp, pl.ds(8 * h + 4 * core, 4), :] = block[4 * h : 4 * h + 4]
+                    spread[pp, pl.ds(8 * h + 4 * core, 4), :] = wall[
+                        core, pp % 4, 2 * q + pp // 8, pp // 4 % 2 * 4 + h
+                    ].astype(F32)
             for half in range(2):
                 rows = [spread[pp, pl.ds(16 * h + half, 8, stride=2), :] for h in range(2)]
                 begin = PIECE * pp + LANES * half
@@ -303,12 +293,12 @@
     werr_store.wait()
     for d in range(4):
         to_core(d).wait_send()
-        to_sibling(d).wait_send()
     for d in range(1, 4):
         to_node(d).wait_send()
-        to_x(d).wait_send()
-    pltpu.make_async_copy(pieces.at[pl.ds(0, everyone)], arrived.at[pl.ds(0, everyone)], b_send).wait()
-    pltpu.make_async_copy(pieces.at[pl.ds(0, everyone)], gathered.at[pl.ds(0, everyone)], c_send).wait()
+    pltpu.make_async_copy(arrived.at[others], arrived.at[others], b_send).wait()
+    pltpu.make_async_copy(arrived.at[others], arrived.at[others], c_send).wait()
+    pltpu.make_async_copy(wall.at[c, pl.ds(0, 3)], wall.at[c, pl.ds(0, 3)], x_send).wait()
+    pltpu.make_async_copy(wall.at[c], wall.at[c], s_send).wait()
 
 
 def finish(*refs):
@@ -350,15 +340,14 @@
             pltpu.VMEM((GROUPS + 4, 2, LANES), F32),
             pltpu.VMEM((4, LANES), F32),
             pltpu.VMEM((PADDED, LANES), F32),
-            pltpu.VMEM((SERVERS, 4, LANES), F32),
-            pltpu.VMEM((SERVERS, 4, LANES), F32),
-            pltpu.VMEM((4, LANES), F32),
-            pltpu.VMEM((SERVERS, 4, LANES), F32),
-            pltpu.VMEM((2, 4, 4 * SERVERS, LANES), BF16),
+            pltpu.VMEM((SERVERS, 4, LANES), BF16),
+            pltpu.VMEM((SERVERS, 4, LANES), BF16),
+            pltpu.VMEM((4, LANES), BF16),
+            pltpu.VMEM((2, 4, 8, 8, 4, LANES), BF16),
             pltpu.VMEM((16, 32, LANES), F32),
             dma((8,)), dma((2,)), dma((4,)), dma((4,)), dma((3,)), dma((3,)),
             pltpu.SemaphoreType.REGULAR,
-            dma, dma, dma, dma, dma((3,)), dma((3,)), dma((4,)), dma((4,)),
+            dma, dma, dma, dma((8,)), dma, dma((3,)), dma, dma,
         ],
         compiler_params=pltpu.CompilerParams(
             collective_id=0, has_side_effects=True, vmem_limit_bytes=60 * 1024 * 1024

time: 47.5 us -> 46.7 us (0.983)
  Pallas kernels: 46.7 us -> 45.9 us
    pallas_call x1, Pallas kernels: 45.8 us -> 45 us  [body(): pl.pallas_call(kernel, out_shape=[pltpu.VMEM((GROUPS, 2, LANES), F32), pl...]
where the time goes in v3:
time: 46.7 us; the launch traced here: 46.5 us
  Pallas kernels  45.9 us (98%)
  between operations  0.64 us (1%)
    pallas_call x1, Pallas kernels, body(): pl.pallas_call(kernel, out_shape=[pltpu.VMEM((GROUPS, 2, LANES), F32), pl...  45 us

profile of v3, /device:TPU:1, one launch (start us, length us, event | category | flops | bytes accessed | tf_op | source)
XLA Modules:
  0.0 46.5 jit_solution(8803499594381696762)
XLA Ops:
  0.6 45.0 %compressed_step.1 = (f32[108,2,128]{2,1,0:T(2,128)S(1)}, f32[108,2,128]{2,1,0:T(2,128)S(1)}, f32[2,216]{1,0:T(2,128)S(1)}, bf16[16,13824]{1,0:T(8,128)(2,1)S(1)}) custom-call(bf16[128,13824]{1,0:T(8,128)(2,1)} %bitcast.22, bf16[16,128]{1,0:T(8,128)(2,1)} %bitcast.27, f32[108,2,128]{2,1,0:T(2,128)} %bitcast.23, f32[108,2,128]{2,1,0:T(2,128)} %bitcast.24, ...), custom_call_target="tpu_custom_call" | custom-call | flops 56623104 | bytes 5000000 | tf_op jit(solution)/shard_map/compressed_step/pallas_call | solution.py:321
  45.6 0.9 %finish.1 = (f32[108,2,128]{2,1,0:T(2,128)}, f32[108,2,128]{2,1,0:T(2,128)}, f32[2,216]{1,0:T(2,128)}, bf16[16,13824]{1,0:T(8,128)(2,1)}) custom-call(f32[108,2,128]{2,1,0:T(2,128)S(1)} %get-tuple-element.12.refs_0_, f32[108,2,128]{2,1,0:T(2,128)S(1)} %get-tuple-element.13.refs_1_, f32[2,216]{1,0:T(2,128)S(1)} %get-tuple-element.14.refs_2_, ...), custom_call_target="tpu_custom_call" | custom-call | tf_op jit(solution)/shard_map/finish/pallas_call | solution.py:367

commit v4 on v3

--- a/solution.py
+++ b/solution.py
@@ -36,7 +36,7 @@
 def kernel(
     hid, cot, mom, werr, serr, mast, second,
     moment_out, werr_out, serr_out, weights_out,
-    hid_v, part, core_in, y_out, y_in, mom_v, werr_v, mast_v, second_v, serr_v,
+    cot_v, serr_raw, hid_v, part, core_out, core_in, y_out, y_in, mom_v, werr_v, mast_v, second_v, serr_v,
     sent_v, pieces, arrived, wpiece, wall, spread,
     load_sem, store_sem, core_send, core_recv, y_send, y_recv, ready,
     b_send, b_recv, c_send, c_recv, x_send, x_recv, s_send, s_recv,
@@ -64,27 +64,27 @@
         pltpu.make_async_copy(werr.reshape(DENSE, LANES), werr_v.at[pl.ds(0, DENSE)], load_sem.at[5]),
         pltpu.make_async_copy(mast, mast_v.at[pl.ds(0, GROUPS)], load_sem.at[6]),
         pltpu.make_async_copy(second, second_v.at[pl.ds(0, GROUPS)], load_sem.at[7]),
+        pltpu.make_async_copy(serr, serr_raw, load_sem.at[8]),
     ]
+    barrier = pltpu.get_barrier_semaphore()
+
+    def greet(who):
+        pl.semaphore_signal(barrier, 1, device_id=who, device_id_type=MESH)
+
+    for d in (4, 2, 6):
+        greet(device(x, lax.rem(y + d, 8), z, c))
+    greet(sibling)
+    cot_load = pltpu.make_async_copy(cot, cot_v, load_sem.at[9])
+    cot_load.start()
     for load in loads:
         load.start()
-
-    barrier = pltpu.get_barrier_semaphore()
-
-    def greet(who):
-        pl.semaphore_signal(barrier, 1, device_id=who, device_id_type=MESH)
-
-    @pl.loop(0, 7)
-    def _(j):
-        greet(device(x, y, lax.rem(z + far_first(j, 4), 8), c))
-        greet(device(x, lax.rem(y + far_first(j, 4), 8), z, c))
-
-    @pl.loop(1, 4)
-    def _(j):
-        other = lax.rem(x + j, 4)
-        greet(device(other, y, z, c))
-        greet(device(other, yh * 2 + 1 - yl, z, c))
-
-    greet(sibling)
+    for d in (4, 3, 5, 2, 6, 1, 7):
+        greet(device(x, y, lax.rem(z + d, 8), c))
+    for d in (3, 5, 1, 7):
+        greet(device(x, lax.rem(y + d, 8), z, c))
+    for d in (2, 1, 3):
+        greet(device(lax.rem(x + d, 4), yh * 2 + 1 - yl, z, c))
+        greet(device(lax.rem(x + d, 4), y, z, c))
 
     for state in states:
         state.start()
@@ -98,10 +98,9 @@
     mast_v[pl.ds(GROUPS, 4)] = jnp.zeros((4, 2, LANES), F32)
     second_v[pl.ds(GROUPS, 4)] = jnp.zeros((4, 2, LANES), F32)
     serr_v[...] = jnp.zeros((4, LANES), F32)
-    serr_v[pl.ds(0, 2), :] = serr[:, pl.ds(0, LANES)]
-    serr_v[pl.ds(2, 2), pl.ds(0, PIECE - LANES)] = serr[:, pl.ds(LANES, PIECE - LANES)]
-
-    cot_value = cot[...]
+
+    cot_load.wait()
+    cot_value = cot_v[...]
     for j in range(4):
         loads[j].wait()
         sums = jnp.dot(
@@ -116,11 +115,13 @@
                     2 * n : 2 * n + 2, g * LANES : (g + 1) * LANES
                 ]
 
+    for d in range(4):
+        core_out[d] = part[1 - c, lax.rem(yh + d, 4)].astype(BF16)
     pl.semaphore_wait(barrier, 21)
 
     def to_core(d):
         return pltpu.make_async_remote_copy(
-            part.at[1 - c, lax.rem(yh + d, 4)], core_in.at[d], core_send.at[d], core_recv.at[d],
+            core_out.at[d], core_in.at[d], core_send.at[d], core_recv.at[d],
             device_id=sibling, device_id_type=MESH,
         )
 
@@ -133,18 +134,16 @@
     for d in (2, 1, 3, 0):
         to_core(d).start()
 
-    @pl.loop(0, 7)
-    def _(j):
-        pl.semaphore_signal(
-            ready, 1, device_id=device(x, y, lax.rem(z + far_first(j, 4), 8), c), device_id_type=MESH
-        )
-
     for d in (2, 1, 3):
         to_core(d).wait_recv()
-        y_out[d - 1] = (part[c, lax.rem(yh + d, 4)] + core_in[d]).astype(BF16)
+        y_out[d - 1] = (part[c, lax.rem(yh + d, 4)] + core_in[d].astype(F32)).astype(BF16)
         to_node(d).start()
+    for d in (4, 3, 5, 2, 6, 1, 7):
+        pl.semaphore_signal(
+            ready, 1, device_id=device(x, y, lax.rem(z + d, 8), c), device_id_type=MESH
+        )
     to_core(0).wait_recv()
-    gradient = part[c, yh] + core_in[0]
+    gradient = part[c, yh] + core_in[0].astype(F32)
     states[0].wait()
     states[1].wait()
     for d in (1, 3, 2):
@@ -193,6 +192,9 @@
 
     states[2].wait()
     states[3].wait()
+    states[4].wait()
+    serr_v[pl.ds(0, 2), :] = serr_raw[:, pl.ds(0, LANES)]
+    serr_v[pl.ds(2, 2), pl.ds(0, PIECE - LANES)] = serr_raw[:, pl.ds(LANES, PIECE - LANES)]
     column = dp * PIECE
     group, shift = column // LANES, lax.rem(column, LANES)
 
@@ -326,12 +328,15 @@
             pltpu.VMEM((2, PIECE), F32),
             pltpu.VMEM((16, FF), BF16),
         ],
-        in_specs=[anywhere, vmem, anywhere, anywhere, vmem, anywhere, anywhere],
+        in_specs=[anywhere] * 7,
         out_specs=[anywhere, anywhere, vmem, vmem],
         scratch_shapes=[
+            pltpu.VMEM((16, 128), BF16),
+            pltpu.VMEM((2, PIECE), F32),
             pltpu.VMEM((128, FF), BF16),
             pltpu.VMEM((2, 4, PADDED, LANES), F32),
-            pltpu.VMEM((4, PADDED, LANES), F32),
+            pltpu.VMEM((4, PADDED, LANES), BF16),
+            pltpu.VMEM((4, PADDED, LANES), BF16),
             pltpu.VMEM((3, PADDED, LANES), BF16),
             pltpu.VMEM((3, PADDED, LANES), BF16),
             pltpu.VMEM((PADDED, LANES), F32),
@@ -345,7 +350,7 @@
             pltpu.VMEM((4, LANES), BF16),
             pltpu.VMEM((2, 4, 8, 8, 4, LANES), BF16),
             pltpu.VMEM((16, 32, LANES), F32),
-            dma((8,)), dma((2,)), dma((4,)), dma((4,)), dma((3,)), dma((3,)),
+            dma((10,)), dma((2,)), dma((4,)), dma((4,)), dma((3,)), dma((3,)),
             pltpu.SemaphoreType.REGULAR,
             dma, dma, dma, dma((8,)), dma, dma((3,)), dma, dma,
         ],

time: 46.7 us -> 46 us (0.985)
  Pallas kernels: 45.9 us -> 45.2 us
    pallas_call x1, Pallas kernels: 45 us -> 44.4 us  [body(): pl.pallas_call(kernel, out_shape=[pltpu.VMEM((GROUPS, 2, LANES), F32), pl...]
where the time goes in v4:
time: 46 us; the launch traced here: 45.9 us
  Pallas kernels  45.2 us (98%)
  between operations  0.64 us (1%)
    pallas_call x1, Pallas kernels, body(): pl.pallas_call(kernel, out_shape=[pltpu.VMEM((GROUPS, 2, LANES), F32), pl...  44.4 us

profile of v4, /device:TPU:1, one launch (start us, length us, event | category | flops | bytes accessed | tf_op | source)
XLA Modules:
  0.0 45.9 jit_solution(976833540239519255)
XLA Ops:
  0.6 44.4 %compressed_step.1 = (f32[108,2,128]{2,1,0:T(2,128)S(1)}, f32[108,2,128]{2,1,0:T(2,128)S(1)}, f32[2,216]{1,0:T(2,128)S(1)}, bf16[16,13824]{1,0:T(8,128)(2,1)S(1)}) custom-call(bf16[128,13824]{1,0:T(8,128)(2,1)} %bitcast.22, bf16[16,128]{1,0:T(8,128)(2,1)} %bitcast.27, f32[108,2,128]{2,1,0:T(2,128)} %bitcast.23, f32[108,2,128]{2,1,0:T(2,128)} %bitcast.24, ...), custom_call_target="tpu_custom_call" | custom-call | flops 56623104 | bytes 5000000 | tf_op jit(solution)/shard_map/compressed_step/pallas_call | solution.py:323
  45.0 0.9 %finish.1 = (f32[108,2,128]{2,1,0:T(2,128)}, f32[108,2,128]{2,1,0:T(2,128)}, f32[2,216]{1,0:T(2,128)}, bf16[16,13824]{1,0:T(8,128)(2,1)}) custom-call(f32[108,2,128]{2,1,0:T(2,128)S(1)} %get-tuple-element.12.refs_0_, f32[108,2,128]{2,1,0:T(2,128)S(1)} %get-tuple-element.13.refs_1_, f32[2,216]{1,0:T(2,128)S(1)} %get-tuple-element.14.refs_2_, ...), custom_call_target="tpu_custom_call" | custom-call | tf_op jit(solution)/shard_map/finish/pallas_call | solution.py:372

commit v5 on v4

--- a/solution.py
+++ b/solution.py
@@ -37,7 +37,7 @@
     hid, cot, mom, werr, serr, mast, second,
     moment_out, werr_out, serr_out, weights_out,
     cot_v, serr_raw, hid_v, part, core_out, core_in, y_out, y_in, mom_v, werr_v, mast_v, second_v, serr_v,
-    sent_v, pieces, arrived, wpiece, wall, spread,
+    sent_v, pieces, arrived, wpiece, gathered, wall, spread,
     load_sem, store_sem, core_send, core_recv, y_send, y_recv, ready,
     b_send, b_recv, c_send, c_recv, x_send, x_recv, s_send, s_recv,
 ):
@@ -166,7 +166,7 @@
         if shift:
             first = pltpu.roll(rows, LANES - shift, 1)
             rows = jnp.where(lane < LANES - shift, first, pltpu.roll(first, 6, 0))
-        pieces[p] = rows[0:4].astype(BF16)
+        pieces[p] = rows[0:4]
 
     pl.semaphore_wait(ready, 7)
 
@@ -180,7 +180,7 @@
             pieces.at[target], arrived.at[dp], b_send, b_recv, device_id=(node, target), device_id_type=MESH
         )
 
-    @pl.loop(0, SERVERS - 1, unroll=7)
+    @pl.loop(0, SERVERS - 1, unroll=21)
     def _(k):
         to_server(k).start()
 
@@ -211,14 +211,14 @@
 
     others = pl.ds(0, SERVERS - 1)
     pltpu.make_async_copy(arrived.at[others], arrived.at[others], b_recv).wait()
-    served = jnp.sum(arrived[...].astype(F32), axis=0) / SERVERS + serr_v[...]
+    served = jnp.sum(arrived[...], axis=0) / SERVERS + serr_v[...]
     served = jnp.where(valid, served, 0.0)
     square = jnp.sum(served * served, axis=(0, 1), keepdims=True)
     scale = jnp.sqrt(square / (2 * PIECE) + EPSILON)
     returned = (scale * jnp.tanh(served / scale)).astype(BF16).astype(F32)
     updated = own_master - step * returned
     updated = jnp.concatenate([updated[0:1], updated[2:3], updated[1:2], updated[3:4]], axis=0)
-    wpiece[...] = updated.astype(BF16)
+    wpiece[...] = updated.astype(BF16).astype(F32)
 
     slot = yl * 4 + yh
 
@@ -226,15 +226,15 @@
         dz = far_first(k // 8, 4)
         ty = lax.rem(y + far_first(lax.rem(k, 8), 4), 8)
         return pltpu.make_async_remote_copy(
-            wpiece, wall.at[c, x, z, slot], c_send, c_recv.at[dz],
+            wpiece, gathered.at[z, slot], c_send, c_recv.at[dz],
             device_id=device(x, ty, lax.rem(z + dz, 8), c), device_id_type=MESH,
         )
 
-    @pl.loop(0, SERVERS - 1, unroll=7)
+    @pl.loop(0, SERVERS - 1, unroll=21)
     def _(k):
         to_plane(k).start()
 
-    wall[c, x, z, slot] = wpiece[...]
+    gathered[z, slot] = wpiece[...]
     residual = served - returned
     serr_out[:, pl.ds(0, LANES)] = residual[0:2]
     serr_out[:, pl.ds(LANES, PIECE - LANES)] = residual[2:4, 0 : PIECE - LANES]
@@ -253,8 +253,9 @@
 
     for dz in (0, 1, 7, 2, 6, 3, 5, 4):
         source = lax.rem(z + 8 - dz, 8)
-        landed = wall.at[c, x, source, pl.ds(0, 8 if dz else 7)]
+        landed = gathered.at[source, pl.ds(0, 8 if dz else 7)]
         pltpu.make_async_copy(landed, landed, c_recv.at[dz]).wait()
+        wall[c, x, source] = gathered[source].reshape(32, LANES).astype(BF16)
         for d in (2, 1, 3):
             to_x(d, source).start()
         to_sibling(wall.at[c, x, source]).start()
@@ -269,10 +270,9 @@
         parts = [[] for _ in range(QUARTER)]
         for pp in range(16):
             for core in range(2):
+                block = wall[core, pp % 4, 2 * q + pp // 8, pl.ds(16 * (pp // 4 % 2), 16), :].astype(F32)
                 for h in range(4):
-                    spread[pp, pl.ds(8 * h + 4 * core, 4), :] = wall[
-                        core, pp % 4, 2 * q + pp // 8, pp // 4 % 2 * 4 + h
-                    ].astype(F32)
+                    spread[pp, pl.ds(8 * h + 4 * core, 4), :] = block[4 * h : 4 * h + 4]
             for half in range(2):
                 rows = [spread[pp, pl.ds(16 * h + half, 8, stride=2), :] for h in range(2)]
                 begin = PIECE * pp + LANES * half
@@ -345,10 +345,11 @@
             pltpu.VMEM((GROUPS + 4, 2, LANES), F32),
             pltpu.VMEM((4, LANES), F32),
             pltpu.VMEM((PADDED, LANES), F32),
-            pltpu.VMEM((SERVERS, 4, LANES), BF16),
-            pltpu.VMEM((SERVERS, 4, LANES), BF16),
-            pltpu.VMEM((4, LANES), BF16),
-            pltpu.VMEM((2, 4, 8, 8, 4, LANES), BF16),
+            pltpu.VMEM((SERVERS, 4, LANES), F32),
+            pltpu.VMEM((SERVERS, 4, LANES), F32),
+            pltpu.VMEM((4, LANES), F32),
+            pltpu.VMEM((8, 8, 4, LANES), F32),
+            pltpu.VMEM((2, 4, 8, 32, LANES), BF16),
             pltpu.VMEM((16, 32, LANES), F32),
             dma((10,)), dma((2,)), dma((4,)), dma((4,)), dma((3,)), dma((3,)),
             pltpu.SemaphoreType.REGULAR,

time: 46 us -> 46.7 us (1.015)
  Pallas kernels: 45.2 us -> 45.9 us
    pallas_call x1, Pallas kernels: 44.4 us -> 45.1 us  [body(): pl.pallas_call(kernel, out_shape=[pltpu.VMEM((GROUPS, 2, LANES), F32), pl...]
where the time goes in v5:
time: 46.7 us; the launch traced here: 46.6 us
  Pallas kernels  45.9 us (98%)
  between operations  0.64 us (1%)
    pallas_call x1, Pallas kernels, body(): pl.pallas_call(kernel, out_shape=[pltpu.VMEM((GROUPS, 2, LANES), F32), pl...  45.1 us

profile of v5, /device:TPU:1, one launch (start us, length us, event | category | flops | bytes accessed | tf_op | source)
XLA Modules:
  0.0 46.6 jit_solution(14582548515369148587)
XLA Ops:
  0.6 45.1 %compressed_step.1 = (f32[108,2,128]{2,1,0:T(2,128)S(1)}, f32[108,2,128]{2,1,0:T(2,128)S(1)}, f32[2,216]{1,0:T(2,128)S(1)}, bf16[16,13824]{1,0:T(8,128)(2,1)S(1)}) custom-call(bf16[128,13824]{1,0:T(8,128)(2,1)} %bitcast.22, bf16[16,128]{1,0:T(8,128)(2,1)} %bitcast.27, f32[108,2,128]{2,1,0:T(2,128)} %bitcast.23, f32[108,2,128]{2,1,0:T(2,128)} %bitcast.24, ...), custom_call_target="tpu_custom_call" | custom-call | flops 56623104 | bytes 5000000 | tf_op jit(solution)/shard_map/compressed_step/pallas_call | solution.py:323
  45.7 0.9 %finish.1 = (f32[108,2,128]{2,1,0:T(2,128)}, f32[108,2,128]{2,1,0:T(2,128)}, f32[2,216]{1,0:T(2,128)}, bf16[16,13824]{1,0:T(8,128)(2,1)}) custom-call(f32[108,2,128]{2,1,0:T(2,128)S(1)} %get-tuple-element.12.refs_0_, f32[108,2,128]{2,1,0:T(2,128)S(1)} %get-tuple-element.13.refs_1_, f32[2,216]{1,0:T(2,128)S(1)} %get-tuple-element.14.refs_2_, ...), custom_call_target="tpu_custom_call" | custom-call | tf_op jit(solution)/shard_map/finish/pallas_call | solution.py:373
